TPU v7x, 32 devices: a whole 2x2x4 slice. The times are simulated.
32 devices in a mesh: seq: 4 (over z), shard: 8 (over y, x, core).
Axes of the slice: x: 2, y: 2, z: 4, core: 2. Of those that a mesh axis runs over, the one named last changes fastest.
Arguments:
- tokens: bfloat16 [2, 8, 1024, 768], P(None, 'shard', 'seq'), may hold values from -6 to 6
- segments: int32 [2, 8, 1024], P(None, 'shard', 'seq'), may hold values from 0 to 3, never falling along the last dimension, each value on 1 to 512 neighbouring positions
- w_qkv: bfloat16 [768, 2304], P('shard'), may hold values from -0.21875 to 0.21875
- w_out: bfloat16 [768, 768], P('shard'), may hold values from -2.5 to 2.5
- w_up: bfloat16 [768, 3072], P('shard'), may hold values from -0.21875 to 0.21875
- w_down: bfloat16 [3072, 768], P('shard'), may hold values from -0.109375 to 0.109375
- gain_one: bfloat16 [768], P('shard'), may hold values from 0.5 to 1.5
- gain_two: bfloat16 [768], P('shard'), may hold values from 0.5 to 1.5
- cotangent: bfloat16 [2, 8, 1024, 768], P(None, 'shard', 'seq'), may hold values from -6 to 6
Outputs:
- mixed: bfloat16 [2, 8, 1024, 768], P(None, 'shard', 'seq')
- grad_tokens: float32 [2, 8, 1024, 768], P(None, 'shard', 'seq')
- grad_qkv: float32 [768, 2304], P('shard')
- grad_out: float32 [768, 768], P('shard')
- grad_up: float32 [768, 3072], P('shard')
- grad_down: float32 [3072, 768], P('shard')
- grad_gain_one: float32 [768], P('shard')
- grad_gain_two: float32 [768], P('shard')
Inputs may be any that keep to these rules, and one draw needn't show every extreme that they name: `segments`: within a sequence the ids never decrease; a document spans at most half of 1024 tokens.
All inputs are finite; a program needn't handle non-finite values.
Results may differ from a plain program's by a relative error of at most 0.012.
The roundings to bfloat16 on the way count: a program that leaves them out, or rounds other values in their place, can miss the bound.
Values may be sent and summed in bfloat16 or wider, within the bound.
A program may use at most 192 MiB of HBM per device.

v0:
```python
import functools
import math

import jax
import jax.numpy as jnp
from jax import lax
from jax.experimental import pallas as pl
from jax.experimental.pallas import tpu as pltpu
from jax.sharding import PartitionSpec as P


HEADS = 12
HEAD_DIM = 64


epsilon = 1e-05
far_below = -1e30


def norm_rows(values, gain):
    row_mean = jnp.mean(values, axis=-1, keepdims=True)
    centred = values - row_mean
    spread = jnp.mean(centred * centred, axis=-1, keepdims=True)
    return centred * lax.rsqrt(spread + epsilon) * gain


def gelu_tanh(values):
    return jax.nn.gelu(values, approximate=True)


def product(left, right):
    return jnp.dot(left, right, preferred_element_type=jnp.float32)


def product_left_t(left, right):
    return lax.dot_general(
        left, right, (((0,), (0,)), ((), ())), preferred_element_type=jnp.float32
    )


def product_right_t(left, right):
    return lax.dot_general(
        left, right, (((1,), (1,)), ((), ())), preferred_element_type=jnp.float32
    )


def block_scores(query_block, keys, seg_rows, seg_cols, row_first, score_scale):
    rows_count = query_block.shape[0]
    cols_count = keys.shape[0]
    scores = (
        jnp.einsum("qhd,khd->hqk", query_block, keys, preferred_element_type=jnp.float32)
        * score_scale
    )
    row_pos = row_first + lax.broadcasted_iota(jnp.int32, (rows_count, cols_count), 0)
    col_pos = lax.broadcasted_iota(jnp.int32, (rows_count, cols_count), 1)
    allowed = (col_pos <= row_pos) & (seg_rows[:, None] == seg_cols[None, :])
    return (scores, allowed[None])


def attend_forward(queries, keys, values, seg_all, rows_block, score_scale):
    length = queries.shape[0]
    out_parts = []
    level_parts = []
    for row_first in range(0, length, rows_block):
        query_block = queries[row_first : row_first + rows_block]
        scores, allowed = block_scores(
            query_block,
            keys,
            seg_all[row_first : row_first + rows_block],
            seg_all,
            row_first,
            score_scale,
        )
        magnitude = jnp.abs(scores)
        row_top = jnp.max(jnp.where(allowed, magnitude, far_below), axis=-1, keepdims=True)
        exp_raw = jnp.where(allowed, jnp.exp(magnitude - row_top), 0.0)
        total = jnp.sum(exp_raw, axis=-1, keepdims=True)
        floor_term = jnp.where(allowed, jnp.exp(-row_top), 0.0)
        signed = (jnp.sign(scores) * (exp_raw - floor_term) / total).astype(jnp.bfloat16)
        out_parts.append(
            jnp.einsum("hqk,khd->qhd", signed, values, preferred_element_type=jnp.float32)
        )
        level_parts.append(row_top + jnp.log(total))
    return (jnp.concatenate(out_parts, axis=0), jnp.concatenate(level_parts, axis=1))


def attend_backward(queries, keys, values, seg_all, levels, d_heads, rows_block, score_scale):
    length = queries.shape[0]
    grad_keys = jnp.zeros(keys.shape, jnp.float32)
    grad_values = jnp.zeros(values.shape, jnp.float32)
    query_parts = []
    for row_first in range(0, length, rows_block):
        query_block = queries[row_first : row_first + rows_block]
        d_block = d_heads[row_first : row_first + rows_block]
        scores, allowed = block_scores(
            query_block,
            keys,
            seg_all[row_first : row_first + rows_block],
            seg_all,
            row_first,
            score_scale,
        )
        level_block = levels[:, row_first : row_first + rows_block]
        sign_part = jnp.sign(scores)
        prob = jnp.where(allowed, jnp.exp(jnp.abs(scores) - level_block), 0.0)
        weight = sign_part * jnp.where(allowed, prob - jnp.exp(-level_block), 0.0)
        d_signed = jnp.einsum("qhd,khd->hqk", d_block, values, preferred_element_type=jnp.float32)
        delta = jnp.sum(weight * d_signed, axis=-1, keepdims=True)
        d_score = (prob * (d_signed - sign_part * delta)).astype(jnp.bfloat16)
        query_parts.append(
            jnp.einsum("hqk,khd->qhd", d_score, keys, preferred_element_type=jnp.float32)
            * score_scale
        )
        grad_keys = (
            grad_keys
            + jnp.einsum("hqk,qhd->khd", d_score, query_block, preferred_element_type=jnp.float32)
            * score_scale
        )
        grad_values = grad_values + jnp.einsum(
            "hqk,qhd->khd", weight.astype(jnp.bfloat16), d_block, preferred_element_type=jnp.float32
        )
    grad_queries = jnp.concatenate(query_parts, axis=0)
    stacked = jnp.stack([grad_queries, grad_keys, grad_values], axis=1)
    heads_dev = queries.shape[1]
    return stacked.astype(jnp.bfloat16).reshape(length, 3, 1, heads_dev * queries.shape[2])


def per_device(tokens, segments, w_qkv, w_out, w_up, w_down, gain_one, gain_two, cotangent):
    micro_count = tokens.shape[0]
    tok_rows = tokens.shape[2]
    width = tokens.shape[3]
    groups = lax.axis_size("seq")
    heads_dev = HEADS // groups
    head_cols = heads_dev * HEAD_DIM
    length = tok_rows * groups
    rows_block = min(512, length)
    score_scale = HEAD_DIM ** (-0.5)
    totals = None
    shares = None
    results = []
    grad_rows = []
    for micro_idx in range(micro_count):
        whole = (
            lax.all_gather(w_qkv, "shard", axis=0, tiled=True),
            lax.all_gather(w_out, "shard", axis=0, tiled=True),
            lax.all_gather(w_up, "shard", axis=0, tiled=True),
            lax.all_gather(w_down, "shard", axis=0, tiled=True),
            lax.all_gather(gain_one, "shard", axis=0, tiled=True),
            lax.all_gather(gain_two, "shard", axis=0, tiled=True),
        )
        full_qkv, full_out, full_up, full_down = (whole[0], whole[1], whole[2], whole[3])
        gain_first = whole[4].astype(jnp.float32)
        gain_second = whole[5].astype(jnp.float32)
        tokens_f = tokens[micro_idx, 0].astype(jnp.float32)
        seg_local = segments[micro_idx, 0].astype(jnp.bfloat16)
        normed = norm_rows(tokens_f, gain_first).astype(jnp.bfloat16)
        packed = (
            product(normed, full_qkv).astype(jnp.bfloat16).reshape(tok_rows, 3, groups, head_cols)
        )
        seg_tile = jnp.broadcast_to(seg_local[:, None, None, None], (tok_rows, 1, groups, 1))
        received, seg_recv = (
            lax.all_to_all(packed, "seq", split_axis=2, concat_axis=0, tiled=True),
            lax.all_to_all(seg_tile, "seq", split_axis=2, concat_axis=0, tiled=True),
        )
        queries = received[:, 0, 0].reshape(length, heads_dev, HEAD_DIM)
        keys = received[:, 1, 0].reshape(length, heads_dev, HEAD_DIM)
        values = received[:, 2, 0].reshape(length, heads_dev, HEAD_DIM)
        seg_all = seg_recv[:, 0, 0, 0]
        heads_out, levels = attend_forward(queries, keys, values, seg_all, rows_block, score_scale)
        heads_low = heads_out.astype(jnp.bfloat16).reshape(length, 1, head_cols)
        attended = lax.all_to_all(
            heads_low, "seq", split_axis=0, concat_axis=1, tiled=True
        ).reshape(tok_rows, width)
        middle = tokens_f + product(attended, full_out)
        normed_two = norm_rows(middle, gain_second).astype(jnp.bfloat16)
        up_pre = product(normed_two, full_up)
        active = gelu_tanh(up_pre).astype(jnp.bfloat16)
        results.append((middle + product(active, full_down)).astype(jnp.bfloat16))
        again = (
            lax.all_gather(w_qkv, "shard", axis=0, tiled=True),
            lax.all_gather(w_out, "shard", axis=0, tiled=True),
            lax.all_gather(w_up, "shard", axis=0, tiled=True),
            lax.all_gather(w_down, "shard", axis=0, tiled=True),
            lax.all_gather(gain_one, "shard", axis=0, tiled=True),
            lax.all_gather(gain_two, "shard", axis=0, tiled=True),
        )
        back_qkv, back_out, back_up, back_down = (again[0], again[1], again[2], again[3])
        cot_low = cotangent[micro_idx, 0]
        grad_down_term = product_left_t(active, cot_low)
        d_active = product_right_t(cot_low, back_down)
        unused_gelu, gelu_pull = jax.vjp(gelu_tanh, up_pre)
        d_up = gelu_pull(d_active)[0].astype(jnp.bfloat16)
        grad_up_term = product_left_t(normed_two, d_up)
        d_norm_two = product_right_t(d_up, back_up)
        unused_second, second_pull = jax.vjp(norm_rows, middle, gain_second)
        d_middle_norm, grad_gain_two_term = second_pull(d_norm_two)
        d_middle = cot_low.astype(jnp.float32) + d_middle_norm
        d_branch = d_middle.astype(jnp.bfloat16)
        grad_out_term = product_left_t(attended, d_branch)
        d_attended = (
            product_right_t(d_branch, back_out)
            .astype(jnp.bfloat16)
            .reshape(tok_rows, groups, head_cols)
        )
        d_heads = lax.all_to_all(d_attended, "seq", split_axis=1, concat_axis=0, tiled=True)
        d_heads = d_heads[:, 0].reshape(length, heads_dev, HEAD_DIM)
        grad_heads = attend_backward(
            queries, keys, values, seg_all, levels, d_heads, rows_block, score_scale
        )
        d_packed = lax.all_to_all(
            grad_heads, "seq", split_axis=0, concat_axis=2, tiled=True
        ).reshape(tok_rows, 3 * width)
        grad_qkv_term = product_left_t(normed, d_packed)
        d_normed = product_right_t(d_packed, back_qkv)
        unused_first, first_pull = jax.vjp(norm_rows, tokens_f, gain_first)
        d_tokens_norm, grad_gain_one_term = first_pull(d_normed)
        grad_rows.append(d_middle + d_tokens_norm)
        terms = (
            grad_qkv_term,
            grad_out_term,
            grad_up_term,
            grad_down_term,
            grad_gain_one_term,
            grad_gain_two_term,
        )
        if totals is None:
            totals = terms
        else:
            totals = tuple((left_term + right_term for left_term, right_term in zip(totals, terms)))
    shares = (
        lax.psum_scatter(totals[0], "shard", scatter_dimension=0, tiled=True),
        lax.psum_scatter(totals[1], "shard", scatter_dimension=0, tiled=True),
        lax.psum_scatter(totals[2], "shard", scatter_dimension=0, tiled=True),
        lax.psum_scatter(totals[3], "shard", scatter_dimension=0, tiled=True),
        lax.psum_scatter(totals[4], "shard", scatter_dimension=0, tiled=True),
        lax.psum_scatter(totals[5], "shard", scatter_dimension=0, tiled=True),
    )
    replicas = lax.psum((shares[0], shares[1], shares[2], shares[3], shares[4], shares[5]), "seq")
    mixed = jnp.stack(results, axis=0)[:, None]
    grad_tokens = jnp.stack(grad_rows, axis=0)[:, None]
    return (
        mixed,
        grad_tokens,
        replicas[0],
        replicas[1],
        replicas[2],
        replicas[3],
        replicas[4],
        replicas[5],
    )


BF = jnp.bfloat16
F32 = jnp.float32
MESH = pl.DeviceIdType.MESH
N_SEMS = 132
SCHEDULE = (
    (0,),
    (6,),
    (),
    (12,),
    (1,),
    (),
    (7,),
    (13, 18,),
    (2,),
    (8, 24,),
    (14, 30,),
    (),
    (3, 19,),
    (),
    (9, 25,),
    (36,),
    (4,),
    (15, 31,),
    (20, 10,),
    (26, 42,),
    (16, 5,),
    (37,),
    (21, 54, 11, 32,),
    (),
    (),
    (27, 43, 60, 38, 17,),
    (33, 22,),
    (55,),
    (39, 44, 28, 48,),
    (61, 34, 23,),
    (66, 56, 49, 62,),
    (67, 29, 45, 50,),
    (40, 68, 35, 57, 41,),
    (63, 46, 51, 58,),
    (69, 47, 64, 59,),
    (52, 65, 70, 53, 71,),
)

HUGE = 3.0e38
GELU_K = math.sqrt(2.0 / math.pi)
GELU_C = 0.044715
LANES = 128


def nt(left, right, precision=None):
    return lax.dot_general(
        left, right, (((1,), (1,)), ((), ())), preferred_element_type=F32, precision=precision
    )


def tn(left, right):
    return lax.dot_general(left, right, (((0,), (0,)), ((), ())), preferred_element_type=F32)


def nn(left, right, precision=None):
    return jnp.dot(left, right, preferred_element_type=F32, precision=precision)


def row_stats(v):
    mean = jnp.mean(v, axis=-1, keepdims=True)
    cen = v - mean
    var = jnp.mean(cen * cen, axis=-1, keepdims=True)
    return cen, lax.rsqrt(var + epsilon)


def norm_back(dn, n, rstd, gain):
    e = dn * gain
    return (e - jnp.mean(e, axis=-1, keepdims=True) - n * jnp.mean(e * n, axis=-1, keepdims=True)) * rstd


def layer_kernel(names, *refs):
    r = dict(zip(names, refs))
    tok, seg, wqkv, wout, wup, wdn, cot = (
        r[k] for k in ("tok", "seg", "wqkv", "wout", "wup", "wdn", "cot")
    )
    ssem, rsem = r["ssem"], r["rsem"]
    width = tok.shape[2]
    quarter = tok.shape[1]
    half = 2 * quarter
    length = 4 * quarter
    rows_dev = wqkv.shape[0]
    rows_chip = 2 * rows_dev
    hcols = width // 2
    pairs = hcols // LANES
    pcols = 3 * LANES
    ffh = wup.shape[1] // 2
    ffb = wdn.shape[0]

    z = lax.axis_index("seq")
    s = lax.axis_index("shard")
    c = lax.rem(s, 2)
    q = lax.div(s, 2)
    x = lax.rem(q, 2)
    y = lax.div(q, 2)
    part = (z, s + 1 - 2 * c)
    nx = (z, s + 2 - 4 * x)
    ny = (z, s + 4 - 8 * y)
    zp = (z + 1 - 2 * lax.rem(z, 2), s)
    zm = (3 - z, s)
    edge = lax.rem(z, 3) == 0
    mid = lax.rem(z, 3) != 0
    qx = q + 1 - 2 * x
    qy = q + 2 - 4 * y
    zh = lax.div(z, 2)
    zk = lax.rem(z, 2)
    own0 = pl.multiple_of(half * c, half)
    oth0 = pl.multiple_of(half * (1 - c), half)

    used = [0]
    ends = []

    def sems(n=1):
        first = used[0]
        used[0] += n
        return first

    def remote(src, dst, i, dev, j=None):
        return pltpu.make_async_remote_copy(
            src_ref=src,
            dst_ref=dst,
            send_sem=ssem.at[i if j is None else j],
            recv_sem=rsem.at[i],
            device_id=dev,
            device_id_type=MESH,
        )

    def send(src, dst, dev):
        copy = remote(src, dst, sems(), dev)
        copy.start()
        ends.append(copy.wait_send)
        return copy

    def wait_in(ref, i):
        pltpu.make_async_copy(ref, ref, rsem.at[i]).wait()

    def rows(ref, start, n, align=16):
        return ref.at[pl.ds(pl.multiple_of(start, align), n), :]

    nd = (z, s + 2 - 4 * x + 4 - 8 * y)
    qd = 3 - q

    peers = [part, nx, ny, nd]
    for dz in range(1, 4):
        zz = lax.rem(z + dz, 4)
        peers += [(zz, s), (zz, s + 1 - 2 * c)]
    bar = pltpu.get_barrier_semaphore()
    for dev in peers:
        pl.semaphore_signal(bar, inc=1, device_id=dev, device_id_type=MESH)
    spread = (
        lax.broadcasted_iota(jnp.int32, (rows_dev, width), 1)
        == lax.broadcasted_iota(jnp.int32, (rows_dev, width), 0) + rows_dev * s
    ).astype(F32)
    gains = r["gains"]
    for k, g in enumerate((r["g1"], r["g2"])):
        vec = jnp.broadcast_to(g[...].astype(F32), (8, rows_dev))
        gains[0, :, k * width : (k + 1) * width] = nn(vec, spread, lax.Precision.HIGHEST)[0:1, :]
    pl.semaphore_wait(bar, len(peers))

    seg_i = sems(4)
    x_i = sems(2)
    c_i = sems(2)

    def to_chip(src, dst, i_recv, i_send, zd, core):
        is_self = (zd == z) & (core == c)
        dev = (zd, s - c + core)

        @pl.when(is_self)
        def _():
            pltpu.make_async_copy(src, dst, rsem.at[i_recv]).start()

        @pl.when(jnp.logical_not(is_self))
        def _():
            remote(src, dst, i_recv, dev, i_send).start()

        def end():
            @pl.when(jnp.logical_not(is_self))
            def _():
                remote(src, dst, i_recv, dev, i_send).wait_send()

        ends.append(end)

    for m in range(2):
        to_chip(tok.at[m], rows(r["xb"], quarter * zk, quarter), x_i + zk, x_i + m, 2 * m + c, zh)

    my = pl.multiple_of(rows_dev * s, 32)
    partner_rows = pl.ds(pl.multiple_of(part[1] * rows_dev, 32), rows_dev)
    my_rows = pl.ds(my, rows_dev)
    local_d = sems()
    local_i = {name: sems() for name in ("q", "o", "u0", "u1")}
    flip_i = {name: sems() for name in ("q", "o", "u0", "u1")}
    W = {"q": r["w_q"], "o": r["w_o"], "u": r["w_u"], "d": r["w_d"]}

    def dcol(start, n):
        return pl.ds(pl.multiple_of(start, LANES), n)

    half_u = ffh // 2

    def cols_of(name):
        return {
            "q": slice(None),
            "o": dcol(c * hcols, hcols),
            "u0": pl.ds(0, half_u),
            "u1": pl.ds(half_u, half_u),
            "d": slice(None),
        }[name]

    def pieces(name, core):
        if name == "q":
            cuts = [(wqkv, t * width + core * hcols, t * hcols, hcols) for t in range(3)]
        elif name == "o":
            cuts = [(wout, core * hcols, core * hcols, hcols)]
        else:
            js = (0, 1) if name == "u0" else (2, 3)
            cuts = [(wup, (2 * j + core) * ffb, j * ffb, ffb) for j in js]
        for src, col, at, n in cuts:
            yield src.at[:, dcol(col, n)], W[name[0]].at[my_rows, dcol(at, n)]

    def block(name, first, n):
        return W[name[0]].at[pl.ds(pl.multiple_of(first, 32), n), cols_of(name)]

    ag = {}

    def flip(name):
        for src, dst in pieces(name, 1 - c):
            remote(src, dst, flip_i[name], part).start()

        def end():
            mine = block(name, my, rows_dev)
            remote(mine, mine, flip_i[name], part).wait_send()

        ends.append(end)

    def keep(name):
        for src, dst in pieces(name, c):
            pltpu.make_async_copy(src, dst, rsem.at[local_i[name]]).start()

    def ag_wait_sent(i, n_rows, name):
        both = W[name[0]].at[pl.ds(0, 2 * n_rows), cols_of(name)]
        ends.append(lambda: remote(both, both, i, nx).wait_send())

    def ag_own(name):
        i = sems()
        ag[name] = i
        for dev in (nx, ny):
            for src, dst in pieces(name, c):
                remote(src, dst, i, dev).start()
        ag_wait_sent(i, rows_chip, name)

    def ag_partner(name):
        his = block(name, part[1] * rows_dev, rows_dev)
        wait_in(his, flip_i[name])
        for dev in (nx, ny):
            remote(his, his, ag[name], dev).start()

    def ag_first(name):
        if name == "d":
            dst = block("d", ffb * q, ffb)
            i = sems()
            ag["d"] = i
            for dev in (nx, ny):
                remote(wdn, dst, i, dev).start()
            ag_wait_sent(i, ffb, "d")
        else:
            wait_in(block(name, my, rows_dev), local_i[name])
            wait_in(block(name, part[1] * rows_dev, rows_dev), flip_i[name])
            i = sems()
            ag[name] = i
            for dev in (nx, ny):
                for first in (0, third_z):
                    rows_out = block(name, rows_chip * q + first, third)
                    remote(rows_out, rows_out, i, dev).start()
            ag_wait_sent(i, 2 * third, name)

    third = rows_chip // 3
    third_z = third * (1 + zk)

    def ag_second_u(name):
        wait_in(W["u"].at[pl.ds(0, 4 * third), cols_of(name)], ag[name])
        i, iz = sems(), sems()
        ag[name] = (i, iz)
        bx = block(name, rows_chip * qx, third)
        by = block(name, rows_chip * qy + third_z, third)
        remote(bx, bx, i, ny).start()
        remote(by, by, i, nx).start()
        ag_wait_sent(i, third, name)
        for qq in (qx, qy):
            rows_out = block(name, rows_chip * qq + third_z, third)
            remote(rows_out, rows_out, iz, zp).start()

    def ag_third_u(name):
        i, iz = ag[name]
        wait_in(W["u"].at[pl.ds(0, 2 * third), cols_of(name)], i)
        rows_out = block(name, rows_chip * qd + third_z, third)
        remote(rows_out, rows_out, iz, zp).start()
        all_three = W["u"].at[pl.ds(0, 3 * third), cols_of(name)]
        ends.append(lambda: remote(all_three, all_three, iz, zp).wait_send())

    def ag_last_u(name):
        wait_in(W["u"].at[pl.ds(0, 3 * third), cols_of(name)], ag[name][1])

    def ag_second(name):
        full = ffb if name == "d" else rows_chip
        n = full // 2
        wait_in(W[name[0]].at[pl.ds(0, 2 * full), cols_of(name)], ag[name])
        i = sems()
        ag[name] = (i,)
        bx = block(name, full * qx, n)
        by = block(name, full * qy + n, n)
        remote(bx, bx, i, ny).start()
        remote(by, by, i, nx).start()
        ag_wait_sent(i, n, name)

    def ag_last(name):
        full = ffb if name == "d" else rows_chip
        wait_in(block(name, full * qd, full), ag[name][0])
        if name != "d":
            wait_in(block(name, my, rows_dev), local_i[name])

    flip("q")
    ag_own("q")
    g_core = send(gains.at[0], gains.at[1], part)
    flip("o")
    ag_partner("q")
    ag_own("o")
    keep("q")
    keep("o")
    flip("u0")
    flip("u1")
    for m in range(2):
        for core in range(2):
            to_chip(seg.at[m], r["segs"].at[z], seg_i + z, seg_i + 2 * m + core, 2 * m + c, core)
    ag_partner("o")
    keep("u0")
    keep("u1")
    pltpu.make_async_copy(wdn, rows(W["d"], ffb * q, ffb), rsem.at[local_d]).start()

    g_core.wait_recv()
    gains[2] = gains[0] + gains[1]
    g_in = [send(gains.at[2], gains.at[3 + i], dev) for i, dev in enumerate((nx, ny, nd))]
    ag_second("q")
    ag_first("u0")
    ag_first("u1")
    for copy in g_in:
        copy.wait_recv()
    g_all = jnp.where(x == 0, gains[2], gains[3]) + jnp.where(x == 0, gains[3], gains[2])
    g_all = g_all + (gains[4] + gains[5])
    gains[6] = g_all
    gain_one = gains[6][:, :width]
    gain_two = gains[6][:, width:]

    segs, segc, mask = r["segs"], r["segc"], r["mask"]
    for b in range(4):
        wait_in(segs.at[b], seg_i + b)
    for b in range(4):
        tile = jnp.broadcast_to(segs[b].astype(F32), (LANES, quarter))
        segc[pl.ds(quarter * b, quarter), :] = jnp.transpose(tile)
    base = []
    at = 0
    for b in range(4):
        k0 = max(0, b - 2)
        base.append((at, k0, (b - k0 + 1) * quarter))
        for kb in range(k0, b + 1):
            col = segc[pl.ds(quarter * kb, quarter), :]
            same = jnp.concatenate([col] * (quarter // LANES), axis=1) == segs[b].astype(F32)
            if kb == b:
                shape = (quarter, quarter)
                same = same & (
                    lax.broadcasted_iota(jnp.int32, shape, 0)
                    <= lax.broadcasted_iota(jnp.int32, shape, 1)
                )
            mask[pl.ds(at, quarter), :] = jnp.where(same, 1.0, 0.0)
            at += quarter

    xb, normed = r["xb"], r["normed"]
    n_copies = []
    for k in range(2):
        wait_in(rows(xb, quarter * k, quarter), x_i + k)
        cen, rstd = row_stats(xb[pl.ds(quarter * k, quarter), :].astype(F32))
        normed[pl.ds(own0 + quarter * k, quarter), :] = (cen * rstd * gain_one).astype(BF)
        mine = rows(normed, own0 + quarter * k, quarter)
        n_copies.append(send(mine, mine, part))

    ag_last("q")
    qkv = r["qkv"]

    def qkv_rows(first):
        def step(k, _):
            ts = pl.ds(pl.multiple_of(first + quarter * k, quarter), quarter)
            qkv[ts, :] = nn(normed[ts, :], W["q"][...]).astype(BF)
            return 0

        lax.fori_loop(0, 2, step, 0)

    qkv_rows(own0)
    for copy in n_copies:
        copy.wait_recv()
    qkv_rows(oth0)
    ag_second("o")

    attended, lev = r["attended"], r["lev"]
    lane = lax.broadcasted_iota(jnp.int32, (1, LANES), 1)
    head_lane = [jnp.where(lane < LANES // 2, 1.0, 0.0), jnp.where(lane < LANES // 2, 0.0, 1.0)]
    head_bf = [v.astype(BF) for v in head_lane]
    scale = HEAD_DIM ** (-0.5)

    def attend(p):
        for b in range(4):
            at, k0, n = base[b]
            qs = pl.ds(quarter * b, quarter)
            ks = pl.ds(quarter * k0, n)
            query = qkv[qs, dcol(p * LANES, LANES)] * jnp.asarray(scale, BF)
            key = qkv[ks, dcol(hcols + p * LANES, LANES)]
            value = qkv[ks, dcol(2 * hcols + p * LANES, LANES)]
            allowed = mask[pl.ds(at, n), :]
            total_out = None
            for h in range(2):
                sm = nt(key, query * head_bf[h]) * allowed
                mag = jnp.abs(sm)
                top = jnp.max(mag, axis=0, keepdims=True)
                raw = jnp.exp(mag - top)
                low = jnp.exp(-top)
                total = jnp.sum(raw * allowed, axis=0, keepdims=True)
                sign = jnp.clip(sm * HUGE, -1.0, 1.0)
                signed = (sign * (raw - low) * (1.0 / total)).astype(BF)
                lev[2 * p + h, :, qs] = top + jnp.log(total)
                out = tn(signed, value * head_bf[h])
                total_out = out if total_out is None else total_out + out
            attended[qs, dcol(c * hcols + p * LANES, LANES)] = total_out.astype(BF)

    att_i = sems(pairs)

    def att_copy(p):
        cols = attended.at[:, dcol(c * hcols + p * LANES, LANES)]
        return remote(cols, cols, att_i + p, part)

    for p in range(pairs):
        attend(p)
        att_copy(p).start()
        ends.append(att_copy(p).wait_send)
        if p == 0:
            ag_second_u("u0")
            ag_last("o")
            half_o = W["o"].at[:, dcol(c * hcols, hcols)]
            o_copy = send(half_o, half_o, part)
        if p == 1:
            ag_second_u("u1")
            ag_third_u("u0")
            ag_first("d")
        if p == 2:
            ag_third_u("u1")
            for m in range(2):
                dst = rows(r["cb"], quarter * z, quarter)
                to_chip(cot.at[m], dst, c_i + zk, c_i + m, 2 * m + c, zh)
    o_copy.wait_recv()
    for p in range(pairs):
        att_copy(p).wait_recv()

    middle, n2 = r["middle"], r["n2"]
    n2_copies = []
    for k in range(2):
        ts = pl.ds(own0 + quarter * k, quarter)
        ls = pl.ds(quarter * k, quarter)
        mid_v = xb[ls, :].astype(F32) + nn(attended[ts, :], W["o"][...])
        middle[ls, :] = mid_v
        cen, rstd = row_stats(mid_v)
        n2[ts, :] = (cen * rstd * gain_two).astype(BF)
        mine = rows(n2, own0 + quarter * k, quarter)
        n2_copies.append(send(mine, mine, part))

    active, du = r["active"], r["du"]
    ft = 256
    nft = half_u // ft

    def up_rows(first, col):
        def step(i, _):
            ts = pl.ds(first + quarter * lax.div(i, nft), quarter)
            cols = dcol(col + ft * lax.rem(i, nft), ft)
            u = nn(n2[ts, :], W["u"][:, cols])
            u2 = u * u
            t = jnp.tanh(GELU_K * (u + GELU_C * u * u2))
            active[ts, cols] = (0.5 * u * (1.0 + t)).astype(BF)
            slope = 0.5 * (1.0 + t) + 0.5 * u * (1.0 - t * t) * (
                GELU_K * (1.0 + 3.0 * GELU_C * u2)
            )
            du[ts, cols] = slope.astype(BF)
            return 0

        lax.fori_loop(0, 2 * nft, step, 0)

    ag_last_u("u0")
    up_rows(own0, 0)
    for copy in n2_copies:
        copy.wait_recv()
    up_rows(oth0, 0)
    ag_last_u("u1")
    up_rows(own0, half_u)
    ag_second("d")
    wait_in(rows(W["d"], ffb * q, ffb), local_d)
    up_rows(oth0, half_u)

    def reduce_unit(name, ref, stride, off, n, cols, place):
        h2 = n // 2
        r1, r2, r3, r4 = (r[name + k] for k in ("1", "2", "3", "4"))
        fin = r3
        i1, i2, i3, i4 = sems(), sems(), sems(), sems()

        def at_rows(qq, first, count):
            return pl.ds(pl.multiple_of(qq * stride + off + first, 16), count), cols

        def q_of(yy, xx):
            return 2 * yy + xx

        def first():
            for k in range(2):
                remote(ref.at[at_rows(q_of(k, 1 - x), 0, h2)], r1.at[k], i1, nx).start()
                remote(ref.at[at_rows(q_of(1 - y, k), h2, h2)], r1.at[2 + k], i1, ny).start()
            ends.append(lambda: remote(r1, r1, i1, nx).wait_send())

        def second():
            wait_in(r1, i1)
            ra = at_rows(q_of(1 - y, x), 0, h2)
            ref[ra] = (ref[ra].astype(F32) + r1[1 - y].astype(F32)).astype(BF)
            remote(ref.at[ra], r2.at[0], i2, ny).start()
            rb = at_rows(q_of(y, 1 - x), h2, h2)
            ref[rb] = (ref[rb].astype(F32) + r1[3 - x].astype(F32)).astype(BF)
            remote(ref.at[rb], r2.at[1], i2, nx).start()
            ends.append(lambda: remote(r2, r2, i2, nx).wait_send())

        own = at_rows(q, 0, n)

        def third():
            wait_in(r2, i2)
            ra = at_rows(q, 0, h2)
            ref[ra] = (
                ref[ra].astype(F32) + r1[y].astype(F32) + r2[0].astype(F32)
            ).astype(BF)
            rb = at_rows(q, h2, h2)
            ref[rb] = (
                ref[rb].astype(F32) + r1[2 + x].astype(F32) + r2[1].astype(F32)
            ).astype(BF)

            @pl.when(edge)
            def _():
                remote(ref.at[own], r3, i3, zp).start()

        def fourth():
            @pl.when(mid)
            def _():
                wait_in(r3, i3)
                ref[own] = (ref[own].astype(F32) + r3[...].astype(F32)).astype(BF)
                remote(ref.at[own], r4, i4, zm).start()

        def fifth():
            @pl.when(mid)
            def _():
                wait_in(r4, i4)
                fin[...] = (ref[own].astype(F32) + r4[...].astype(F32)).astype(BF)
                remote(fin, fin, i3, zp).start()

        def last():
            @pl.when(edge)
            def _():
                wait_in(fin, i3)

            place(fin)

        def end():
            remote(ref.at[own], r3, i3, zp).wait_send()

            @pl.when(mid)
            def _():
                remote(ref.at[own], r4, i4, zm).wait_send()

        ends.append(end)
        return first, second, third, fourth, fifth, last

    waits = []

    def put(src, dst):
        i = sems()
        copy = pltpu.make_async_copy(src, dst, rsem.at[i])
        copy.start()
        waits.append(copy.wait)

    def by_core(fin, cuts, out):
        i_mine, i_his = sems(), sems()
        mine = pl.ds(pl.multiple_of(c * rows_dev, 32), rows_dev)
        his = pl.ds(pl.multiple_of((1 - c) * rows_dev, 32), rows_dev)
        for src_col, dst_col, n in cuts:
            src, dst = fin.at[his, pl.ds(src_col, n)], out.at[:, dcol(dst_col, n)]
            remote(src, dst, i_his, part).start()
            pltpu.make_async_copy(fin.at[mine, pl.ds(src_col, n)], dst, rsem.at[i_mine]).start()
        whole = fin.at[mine]
        waits.append(lambda: wait_in(whole, i_mine))
        waits.append(lambda: wait_in(whole, i_his))
        ends.append(lambda: remote(whole, whole, i_his, part).wait_send())

    def place_d(i, n):
        return lambda fin: put(fin, r["o_down"].at[pl.ds(n * i, n), :])

    def place_u(j):
        return lambda fin: by_core(fin, [(0, (2 * j + c) * ffb, ffb)], r["o_up"])

    def place_o(fin):
        by_core(fin, [(0, c * hcols, hcols)], r["o_out"])

    def place_q(p):
        cuts = [(t * LANES, t * width + c * hcols + p * LANES, LANES) for t in range(3)]
        return lambda fin: by_core(fin, cuts, r["o_qkv"])

    red = {}
    dn_rows = ffb // 4
    for i in range(4):
        name = "d%d" % i
        red[name] = reduce_unit(
            name, r["g_d"], ffb, dn_rows * i, dn_rows, slice(None), place_d(i, dn_rows)
        )
    for j in range(4):
        name = "u%d" % j
        red[name] = reduce_unit(
            name, r["g_u"], rows_chip, 0, rows_chip, pl.ds(ffb * j, ffb), place_u(j)
        )
    red["o"] = reduce_unit("o", r["g_o"], rows_chip, 0, rows_chip, slice(None), place_o)
    units = list(red)
    units += ["q%d" % p for p in range(pairs)]
    for p in range(pairs):
        name = "q%d" % p
        red[name] = reduce_unit(
            name, r["g_q"].at[p], rows_chip, 0, rows_chip, slice(None), place_q(p)
        )

    turn = iter(SCHEDULE)

    def stages():
        for at in next(turn):
            red[units[at // 6]][at % 6]()

    xs, xr, mixacc = r["xs"], r["xr"], r["mixacc"]

    def down(blk, first, into, fresh):
        w_rows = pl.ds(pl.multiple_of(ffb * blk, LANES), ffb)
        for k in range(2):
            ls = pl.ds(quarter * k, quarter)
            out = nn(active[pl.ds(first + quarter * k, quarter), dcol(ffb * blk, ffb)], W["d"][w_rows, :])
            into[ls, :] = out if fresh else into[ls, :] + out

    for i, blk in enumerate((q, qx, qy)):
        down(blk, oth0, xs.at[1], i == 0)
    ag_last("d")
    down(qd, oth0, xs.at[1], False)
    mix_copies = [
        send(xs.at[1, pl.ds(quarter * k, quarter), :], xr.at[1, pl.ds(quarter * k, quarter), :], part)
        for k in range(2)
    ]
    cb = r["cb"]
    c_copies = []
    for k in range(2):
        mine = rows(cb, own0 + quarter * k, quarter)
        wait_in(mine, c_i + k)
        c_copies.append(send(mine, mine, part))
    for k in range(2):
        ls = pl.ds(quarter * k, quarter)
        mixacc[ls, :] = nn(active[pl.ds(own0 + quarter * k, quarter), :], W["d"][...])

    def from_chip(buf, out, i0, k):
        zd = 2 * c + k
        src = buf.at[pl.ds(quarter * k, quarter), :]
        is_self = (zd == z) & (zk == c)
        dev = (zd, s - c + zk)
        dst = out.at[zh]

        @pl.when(is_self)
        def _():
            pltpu.make_async_copy(src, dst, rsem.at[i0 + zh]).start()

        @pl.when(jnp.logical_not(is_self))
        def _():
            remote(src, dst, i0 + zh, dev, i0 + k).start()

        def end():
            @pl.when(jnp.logical_not(is_self))
            def _():
                remote(src, dst, i0 + zh, dev, i0 + k).wait_send()

        ends.append(end)
        waits.append(functools.partial(wait_in, out.at[k], i0 + k))

    mo_i, to_i = sems(2), sems(2)
    mixb = r["mixb"]
    for k in range(2):
        ls = pl.ds(quarter * k, quarter)
        mix_copies[k].wait_recv()
        mixb[ls, :] = (middle[ls, :] + mixacc[ls, :] + xr[1, ls, :]).astype(BF)
        from_chip(mixb, r["o_mixed"], mo_i, k)

    for copy in c_copies:
        copy.wait_recv()
    gt = 256

    def grad_down_step(i, _):
        cols = dcol(gt * i, gt)
        r["g_d"][pl.ds(pl.multiple_of(gt * i, gt), gt), :] = tn(active[:, cols], cb[...]).astype(BF)
        return 0

    lax.fori_loop(0, ffh // gt, grad_down_step, 0)
    stages()

    fd = 512

    for k in range(4):

        def d_up_step(i, _):
            ts = pl.ds(quarter * k, quarter)
            cols = dcol(fd * i, fd)
            da = nt(cb[ts, :], W["d"][pl.ds(pl.multiple_of(fd * i, LANES), fd), :])
            du[ts, cols] = (da * du[ts, cols].astype(F32)).astype(BF)
            return 0

        lax.fori_loop(0, ffh // fd, d_up_step, 0)
        stages()

    def exchange(n, product_of):
        copies = []
        for k in range(2):
            ls = pl.ds(quarter * k, quarter)
            xs[n % 2, ls, :] = product_of(pl.ds(oth0 + quarter * k, quarter))
            copies.append(send(xs.at[n % 2, ls, :], xr.at[n % 2, ls, :], part))
        return copies

    dn2_copies = exchange(0, lambda ts: nt(du[ts, :], W["u"][...]))
    stages()
    dbr, gsum = r["dbr"], r["gsum"]
    gain_acc = jnp.zeros((1, width), F32)
    db_copies = []
    for k in range(2):
        ts = pl.ds(own0 + quarter * k, quarter)
        ls = pl.ds(quarter * k, quarter)
        dn = nt(du[ts, :], W["u"][...])
        dn2_copies[k].wait_recv()
        dn = dn + xr[0, ls, :]
        cen, rstd = row_stats(middle[ls, :])
        n = cen * rstd
        gain_acc = gain_acc + jnp.sum(dn * n, axis=0, keepdims=True)
        dmid = cb[ts, :].astype(F32) + norm_back(dn, n, rstd, gain_two)
        mixacc[ls, :] = dmid
        dbr[ts, :] = dmid.astype(BF)
        mine = rows(dbr, own0 + quarter * k, quarter)
        db_copies.append(send(mine, mine, part))
        stages()
    gsum[0, :, width:] = gain_acc

    for j in range(2):

        def grad_up_step(i, _):
            cols = dcol(gt * i, gt)
            out = tn(n2[:, cols], du[:, pl.ds(half_u * j, half_u)]).astype(BF)
            r["g_u"][pl.ds(pl.multiple_of(gt * i, gt), gt), pl.ds(half_u * j, half_u)] = out
            return 0

        lax.fori_loop(0, width // gt, grad_up_step, 0)
        stages()

    for copy in db_copies:
        copy.wait_recv()
    datt = r["datt"]

    def datt_step(k, _):
        ts = pl.ds(pl.multiple_of(quarter * k, quarter), quarter)
        w_rows = W["o"][pl.ds(pl.multiple_of(c * hcols, LANES), hcols), :]
        datt[ts, :] = nt(dbr[ts, :], w_rows).astype(BF)
        return 0

    lax.fori_loop(0, 4, datt_step, 0)
    stages()

    dk, dv = r["dk"], r["dv"]
    sel = (
        lax.broadcasted_iota(jnp.int32, (8, LANES), 0)
        == lax.div(lax.broadcasted_iota(jnp.int32, (8, LANES), 1), LANES // 2)
    ).astype(F32)

    def attend_back(p):
        dk[...] = jnp.zeros_like(dk)
        dv[...] = jnp.zeros_like(dv)
        for b in range(4):
            at, k0, n = base[b]
            qs = pl.ds(quarter * b, quarter)
            ks = pl.ds(quarter * k0, n)
            query = qkv[qs, dcol(p * LANES, LANES)] * jnp.asarray(scale, BF)
            key = qkv[ks, dcol(hcols + p * LANES, LANES)]
            value = qkv[ks, dcol(2 * hcols + p * LANES, LANES)]
            d_att = datt[qs, dcol(p * LANES, LANES)]
            att = attended[qs, dcol(c * hcols + p * LANES, LANES)]
            delta = nt(sel, d_att.astype(F32) * att.astype(F32), lax.Precision.HIGHEST)
            allowed = mask[pl.ds(at, n), :]
            d_query = None
            for h in range(2):
                q_h = query * head_bf[h]
                d_h = d_att * head_bf[h]
                sm = nt(key, q_h) * allowed
                mag = jnp.abs(sm)
                level = lev[2 * p + h, :, qs]
                prob = jnp.exp(mag - level)
                low = jnp.exp(-level)
                sign = jnp.clip(sm * HUGE, -1.0, 1.0)
                weight = (sign * (prob - low)).astype(BF)
                d_signed = nt(value, d_h)
                d_score = (prob * allowed * (d_signed - sign * delta[h : h + 1, :])).astype(BF)
                dv[ks, :] += nn(weight, d_h)
                dk[ks, :] += nn(d_score, q_h)
                out = tn(d_score, key * head_bf[h])
                d_query = out if d_query is None else d_query + out
            qkv[qs, dcol(p * LANES, LANES)] = (d_query * scale).astype(BF)
            stages()
        qkv[:, dcol(hcols + p * LANES, LANES)] = dk[...].astype(BF)
        qkv[:, dcol(2 * hcols + p * LANES, LANES)] = dv[...].astype(BF)

    def grad_qkv(p):
        def step(i, _):
            cols = dcol(gt * i, gt)
            d_pair = jnp.concatenate(
                [qkv[:, dcol(t * hcols + p * LANES, LANES)] for t in range(3)], axis=1
            )
            out = tn(normed[:, cols], d_pair).astype(BF)
            r["g_q"][p, pl.ds(pl.multiple_of(gt * i, gt), gt), :] = out
            return 0

        lax.fori_loop(0, width // gt, step, 0)

    def grad_out_step(i, _):
        cols = dcol(gt * i, gt)
        out = tn(attended[:, cols], dbr[:, dcol(c * hcols, hcols)]).astype(BF)
        r["g_o"][pl.ds(pl.multiple_of(gt * i, gt), gt), :] = out
        return 0

    attend_back(0)
    grad_qkv(0)
    stages()
    attend_back(1)
    grad_qkv(1)
    stages()
    lax.fori_loop(0, width // gt, grad_out_step, 0)
    stages()
    attend_back(2)
    grad_qkv(2)
    stages()

    for copy in dn2_copies:
        copy.wait_send()
        ends.remove(copy.wait_send)
    dn1_copies = exchange(2, lambda ts: nt(qkv[ts, :], W["q"][...]))
    stages()
    gtb = r["gtb"]
    gain_acc = jnp.zeros((1, width), F32)
    for k in range(2):
        ts = pl.ds(own0 + quarter * k, quarter)
        ls = pl.ds(quarter * k, quarter)
        dn = nt(qkv[ts, :], W["q"][...])
        dn1_copies[k].wait_recv()
        dn = dn + xr[0, ls, :]
        cen, rstd = row_stats(xb[ls, :].astype(F32))
        n = cen * rstd
        gain_acc = gain_acc + jnp.sum(dn * n, axis=0, keepdims=True)
        gtb[ls, :] = (mixacc[ls, :] + norm_back(dn, n, rstd, gain_one)).astype(BF)
        from_chip(gtb, r["o_gt"], to_i, k)
        stages()
    gsum[0, :, :width] = gain_acc

    g3, g4, g5 = sems(), sems(), sems()
    g_copy = send(gsum.at[0], gsum.at[1], part)
    stages()

    g_copy.wait_recv()
    gsum[2] = gsum[0] + gsum[1]
    g_copy = send(gsum.at[2], gsum.at[3], nx)
    stages()
    g_copy.wait_recv()
    gsum[4] = gsum[2] + gsum[3]
    g_copy = send(gsum.at[4], gsum.at[5], ny)
    stages()
    g_copy.wait_recv()
    gsum[6] = gsum[4] + gsum[5]

    @pl.when(edge)
    def _():
        remote(gsum.at[6], gsum.at[7], g3, zp).start()

    stages()

    @pl.when(mid)
    def _():
        remote(gsum.at[6], gsum.at[7], g3, zp).wait_recv()
        gsum[8] = gsum[6] + gsum[7]
        remote(gsum.at[8], gsum.at[9], g4, zm).start()

    stages()

    @pl.when(mid)
    def _():
        remote(gsum.at[8], gsum.at[9], g4, zm).wait_recv()
        gsum[10] = gsum[8] + gsum[9]
        remote(gsum.at[10], gsum.at[10], g5, zp).start()

    stages()

    @pl.when(mid)
    def _():
        remote(gsum.at[8], gsum.at[9], g4, zm).wait_send()
        remote(gsum.at[10], gsum.at[10], g5, zp).wait_send()

    @pl.when(edge)
    def _():
        remote(gsum.at[10], gsum.at[10], g5, zp).wait_recv()
        remote(gsum.at[6], gsum.at[7], g3, zp).wait_send()

    pick = (
        lax.broadcasted_iota(jnp.int32, (width, LANES), 0)
        == lax.broadcasted_iota(jnp.int32, (width, LANES), 1) + rows_dev * s
    ).astype(F32)
    for k in range(2):
        vec = jnp.broadcast_to(gsum[10][:, width * k : width * (k + 1)], (8, width))
        r["o_gains"][k : k + 1, :] = nn(vec, pick, lax.Precision.HIGHEST)[0:1, :rows_dev]
    for wait in waits:
        wait()
    for end in ends:
        end()
    assert used[0] <= N_SEMS, used[0]


def per_device_fast(tokens, segments, w_qkv, w_out, w_up, w_down, gain_one, gain_two, cotangent):
    micro, _, quarter, width = tokens.shape
    rows_dev = w_qkv.shape[0]
    ff = w_up.shape[1]
    ffb = w_down.shape[0]
    half, length = 2 * quarter, 4 * quarter
    hcols, ffh, rows_chip = width // 2, ff // 2, 2 * rows_dev
    pairs = hcols // LANES
    pcols = 3 * LANES
    scratch = {}

    def vm(name, shape, dtype=BF):
        scratch[name] = pltpu.VMEM(shape, dtype)

    vm("w_q", (width, pairs * pcols))
    vm("w_o", (width, width))
    vm("w_u", (width, ffh))
    vm("w_d", (ffh, width))
    vm("segs", (4, 1, quarter), jnp.int32)
    vm("segc", (length, LANES), F32)
    vm("mask", (9 * quarter, quarter), F32)
    vm("xb", (half, width))
    vm("cb", (length, width))
    vm("gains", (7, 1, 2 * width), F32)
    vm("gsum", (11, 1, 2 * width), F32)
    vm("normed", (length, width))
    vm("qkv", (length, pairs * pcols))
    vm("lev", (2 * pairs, 1, length), F32)
    vm("attended", (length, width))
    vm("middle", (half, width), F32)
    vm("n2", (length, width))
    vm("active", (length, ffh))
    vm("du", (length, ffh))
    vm("xs", (2, half, width), F32)
    vm("xr", (2, half, width), F32)
    vm("mixb", (half, width))
    vm("mixacc", (half, width), F32)
    vm("gtb", (half, width))
    vm("dbr", (length, width))
    vm("datt", (length, hcols))
    vm("dk", (length, LANES), F32)
    vm("dv", (length, LANES), F32)
    vm("g_d", (ffh, width))
    vm("g_u", (width, ffh))
    vm("g_o", (width, hcols))
    vm("g_q", (pairs, width, pcols))
    pieces = [("d%d" % i, ffb // 4, width) for i in range(4)]
    pieces += [("u%d" % j, rows_chip, ffb) for j in range(4)]
    pieces += [("o", rows_chip, hcols)]
    pieces += [("q%d" % p, rows_chip, pcols) for p in range(pairs)]
    for name, blk, cols in pieces:
        vm(name + "1", (4, blk // 2, cols))
        vm(name + "2", (2, blk // 2, cols))
        vm(name + "3", (blk, cols))
        vm(name + "4", (blk, cols))
    scratch["ssem"] = pltpu.SemaphoreType.DMA((N_SEMS,))
    scratch["rsem"] = pltpu.SemaphoreType.DMA((N_SEMS,))
    outs = {
        "o_mixed": ((micro, quarter, width), BF),
        "o_gt": ((micro, quarter, width), BF),
        "o_qkv": ((rows_dev, 3 * width), BF),
        "o_out": ((rows_dev, width), BF),
        "o_up": ((rows_dev, ff), BF),
        "o_down": ((ffb, width), BF),
        "o_gains": ((2, rows_dev), F32),
    }
    ins = ["tok", "seg", "wqkv", "wout", "wup", "wdn", "g1", "g2", "cot"]
    names = ins + list(outs) + list(scratch)
    hbm = pl.BlockSpec(memory_space=pl.ANY)
    vmem = pl.BlockSpec(memory_space=pltpu.VMEM)
    tokens_all = 2 * half
    flops = 6 * half * (width * (4 * width + 2 * ff)) + 14 * 9 * 6 * quarter * quarter * 128
    got = pl.pallas_call(
        functools.partial(layer_kernel, names),
        out_shape=[jax.ShapeDtypeStruct(*v) for v in outs.values()],
        in_specs=[vmem if k in ("g1", "g2") else hbm for k in ins],
        out_specs=[vmem if k == "o_gains" else hbm for k in outs],
        scratch_shapes=list(scratch.values()),
        compiler_params=pltpu.CompilerParams(
            collective_id=0, has_side_effects=True, vmem_limit_bytes=VMEM_LIMIT
        ),
        cost_estimate=pl.CostEstimate(
            flops=flops, bytes_accessed=20 * tokens_all * width, transcendentals=0
        ),
    )(
        tokens[:, 0],
        segments.reshape(micro, 1, quarter),
        w_qkv,
        w_out,
        w_up,
        w_down,
        gain_one[None],
        gain_two[None],
        cotangent[:, 0],
    )
    mixed, grad_tokens, g_qkv, g_out, g_up, g_down, g_gains = got
    return (
        mixed[:, None],
        grad_tokens.astype(F32)[:, None],
        g_qkv.astype(F32),
        g_out.astype(F32),
        g_up.astype(F32),
        g_down.astype(F32),
        g_gains[0],
        g_gains[1],
    )


VMEM_LIMIT = 62 * 1024 * 1024


def solution(mesh):
    placed = (
        P(None, "shard", "seq", None),
        P(None, "shard", "seq"),
        P("shard", None),
        P("shard", None),
        P("shard", None),
        P("shard", None),
        P("shard"),
        P("shard"),
        P(None, "shard", "seq", None),
    )
    chip_sized = mesh.shape["seq"] == 4 and mesh.shape["shard"] == 8
    return jax.shard_map(
        per_device_fast if chip_sized else per_device,
        mesh=mesh,
        in_specs=placed,
        out_specs=(
            P(None, "shard", "seq", None),
            P(None, "shard", "seq", None),
            P("shard", None),
            P("shard", None),
            P("shard", None),
            P("shard", None),
            P("shard"),
            P("shard"),
        ),
        check_vma=False,
    )
```

profile of v0, /device:TPU:24, one launch (start us, length us, event | category | flops | bytes accessed | tf_op | source)
XLA Modules:
  0.0 172.4 jit_solution(2447282500876039443)
XLA Ops:
  0.6 163.5 %shard_map.152 = (bf16[2,256,768]{2,1,0:T(8,128)(2,1)}, bf16[2,256,768]{2,1,0:T(8,128)(2,1)}, bf16[96,2304]{1,0:T(8,128)(2,1)}, bf16[96,768]{1,0:T(8,128)(2,1)},...) custom-call(bf16[2,256,768]{2,1,0:T(8,128)(2,1)} %bitcast.18, s32[2,1,256]{2,1,0:T(1,128)} %refs_1_.1, ...), custom_call_target="tpu_custom_call" | custom-call | flops 28085059584 | bytes 15728640 | tf_op jit(solution)/shard_map/pallas_call | solution.py:1259
  164.2 0.0 copy-start.3
  164.2 0.0 copy-start.4
  164.2 0.0 copy-start.2
  164.2 2.5 %bitcast_convert_fusion = f32[2,1,256,768]{3,2,1,0:T(8,128)} fusion(bf16[2,256,768]{2,1,0:T(8,128)(2,1)} %get-tuple-element.16), kind=kLoop, calls=%fused_computation | loop fusion | flops 393216 | bytes 2359296
  166.7 0.0 copy-done.3
  166.7 0.0 copy-start.1
  166.7 1.0 convert_element_type.13
  167.6 0.0 copy-done.4
  167.6 0.7 convert_element_type.14
  168.4 0.0 copy-done.2
  168.4 0.0 copy-start.5
  168.4 0.0 copy-start
  168.4 1.1 convert_element_type.15
  169.5 0.0 copy-done.1
  169.5 1.1 convert_element_type.16
  170.6 0.0 copy-done.5
  170.6 0.5 slice_bitcast_fusion
  171.1 0.0 copy-done
  171.1 0.9 copy.20
Async XLA Ops:
  164.2 2.5 %copy-start.3 = (bf16[96,2304]{1,0:T(8,128)(2,1)S(1)}, bf16[96,2304]{1,0:T(8,128)(2,1)}, u32[]{:S(2)}) copy-start(bf16[96,2304]{1,0:T(8,128)(2,1)} %get-tuple-element.17) | copy-start | bytes 1327108
  164.2 3.5 %copy-start.4 = (bf16[96,768]{1,0:T(8,128)(2,1)S(1)}, bf16[96,768]{1,0:T(8,128)(2,1)}, u32[]{:S(2)}) copy-start(bf16[96,768]{1,0:T(8,128)(2,1)} %get-tuple-element.18) | copy-start | bytes 442372
  164.2 4.2 %copy-start.2 = (bf16[96,3072]{1,0:T(8,128)(2,1)S(1)}, bf16[96,3072]{1,0:T(8,128)(2,1)}, u32[]{:S(2)}) copy-start(bf16[96,3072]{1,0:T(8,128)(2,1)} %get-tuple-element.19) | copy-start | bytes 1769476
  166.7 2.8 %copy-start.1 = (bf16[384,768]{1,0:T(8,128)(2,1)S(1)}, bf16[384,768]{1,0:T(8,128)(2,1)}, u32[]{:S(2)}) copy-start(bf16[384,768]{1,0:T(8,128)(2,1)} %get-tuple-element.20) | copy-start | bytes 1769476
  168.4 2.2 %copy-start.5 = (f32[2,96]{1,0:T(2,128)S(1)}, f32[2,96]{1,0:T(2,128)}, u32[]{:S(2)}) copy-start(f32[2,96]{1,0:T(2,128)} %get-tuple-element.21) | copy-start | bytes 2308
  168.4 2.7 %copy-start = (bf16[2,256,768]{2,1,0:T(8,128)(2,1)S(1)}, bf16[2,256,768]{2,1,0:T(8,128)(2,1)}, u32[]{:S(2)}) copy-start(bf16[2,256,768]{2,1,0:T(8,128)(2,1)} %get-tuple-element.15) | copy-start | bytes 2359300
where the time goes:
time: 176 us; the launch traced here: 172 us
  Pallas kernels  164 us (93%)
  other arithmetic  6.38 us (4%)
    pallas_call x1, Pallas kernels, per_device_fast(): pl.pallas_call(functools.partial(layer_kernel, names), out_shape=[jax.Sha...  164 us

commit v1 on v0

--- a/solution.py
+++ b/solution.py
@@ -257,40 +257,42 @@
 SCHEDULE = (
     (0,),
     (6,),
+    (12, 72, 73,),
+    (1,),
+    (18,),
+    (7,),
     (),
-    (12,),
-    (1,),
+    (13,),
+    (2,),
+    (19,),
+    (8, 24, 30,),
+    (14,),
+    (20, 36,),
     (),
-    (7,),
-    (13, 18,),
-    (2,),
-    (8, 24,),
-    (14, 30,),
+    (3, 25,),
+    (42,),
+    (9, 31,),
     (),
-    (3, 19,),
-    (),
-    (9, 25,),
-    (36,),
-    (4,),
-    (15, 31,),
-    (20, 10,),
-    (26, 42,),
-    (16, 5,),
+    (15, 4,),
     (37,),
-    (21, 54, 11, 32,),
-    (),
-    (),
-    (27, 43, 60, 38, 17,),
-    (33, 22,),
-    (55,),
-    (39, 44, 28, 48,),
-    (61, 34, 23,),
-    (66, 56, 49, 62,),
-    (67, 29, 45, 50,),
-    (40, 68, 35, 57, 41,),
-    (63, 46, 51, 58,),
-    (69, 47, 64, 59,),
-    (52, 65, 70, 53, 71,),
+    (21, 26, 54,),
+    (10,),
+    (43, 5,),
+    (32, 16, 60,),
+    (38,),
+    (27, 22,),
+    (48, 11,),
+    (44, 33, 55, 17,),
+    (28,),
+    (39, 61, 66, 23,),
+    (49, 45, 34, 74,),
+    (56, 29, 75,),
+    (62, 40, 35,),
+    (67, 46, 50, 68,),
+    (57, 41, 63,),
+    (47, 51, 58, 69,),
+    (64, 59, 52,),
+    (65, 70, 53, 71,),
 )
 
 HUGE = 3.0e38
@@ -458,7 +460,8 @@
             "o": dcol(c * hcols, hcols),
             "u0": pl.ds(0, half_u),
             "u1": pl.ds(half_u, half_u),
-            "d": slice(None),
+            "d0": slice(None),
+            "d1": slice(None),
         }[name]
 
     def pieces(name, core):
@@ -509,68 +512,41 @@
         for dev in (nx, ny):
             remote(his, his, ag[name], dev).start()
 
+    half_d = ffb // 2
+
+    def span(name):
+        return half_d if name[0] == "d" else rows_chip
+
+    def chip_rows(name, qq, first, n):
+        base = ffb * qq + half_d * int(name[1]) if name[0] == "d" else rows_chip * qq
+        return block(name, base + first, n)
+
     def ag_first(name):
-        if name == "d":
-            dst = block("d", ffb * q, ffb)
-            i = sems()
-            ag["d"] = i
-            for dev in (nx, ny):
-                remote(wdn, dst, i, dev).start()
-            ag_wait_sent(i, ffb, "d")
-        else:
-            wait_in(block(name, my, rows_dev), local_i[name])
-            wait_in(block(name, part[1] * rows_dev, rows_dev), flip_i[name])
+        if name[0] == "d":
             i = sems()
             ag[name] = i
             for dev in (nx, ny):
-                for first in (0, third_z):
-                    rows_out = block(name, rows_chip * q + first, third)
-                    remote(rows_out, rows_out, i, dev).start()
-            ag_wait_sent(i, 2 * third, name)
-
-    third = rows_chip // 3
-    third_z = third * (1 + zk)
-
-    def ag_second_u(name):
-        wait_in(W["u"].at[pl.ds(0, 4 * third), cols_of(name)], ag[name])
-        i, iz = sems(), sems()
-        ag[name] = (i, iz)
-        bx = block(name, rows_chip * qx, third)
-        by = block(name, rows_chip * qy + third_z, third)
-        remote(bx, bx, i, ny).start()
-        remote(by, by, i, nx).start()
-        ag_wait_sent(i, third, name)
-        for qq in (qx, qy):
-            rows_out = block(name, rows_chip * qq + third_z, third)
-            remote(rows_out, rows_out, iz, zp).start()
-
-    def ag_third_u(name):
-        i, iz = ag[name]
-        wait_in(W["u"].at[pl.ds(0, 2 * third), cols_of(name)], i)
-        rows_out = block(name, rows_chip * qd + third_z, third)
-        remote(rows_out, rows_out, iz, zp).start()
-        all_three = W["u"].at[pl.ds(0, 3 * third), cols_of(name)]
-        ends.append(lambda: remote(all_three, all_three, iz, zp).wait_send())
-
-    def ag_last_u(name):
-        wait_in(W["u"].at[pl.ds(0, 3 * third), cols_of(name)], ag[name][1])
+                src = wdn.at[pl.ds(half_d * int(name[1]), half_d), :]
+                remote(src, chip_rows(name, q, 0, half_d), i, dev).start()
+            ag_wait_sent(i, half_d, name)
+        else:
+            ag_own(name)
+            ag_partner(name)
 
     def ag_second(name):
-        full = ffb if name == "d" else rows_chip
-        n = full // 2
-        wait_in(W[name[0]].at[pl.ds(0, 2 * full), cols_of(name)], ag[name])
+        n = span(name) // 2
+        wait_in(W[name[0]].at[pl.ds(0, 4 * n), cols_of(name)], ag[name])
         i = sems()
         ag[name] = (i,)
-        bx = block(name, full * qx, n)
-        by = block(name, full * qy + n, n)
+        bx = chip_rows(name, qx, 0, n)
+        by = chip_rows(name, qy, n, n)
         remote(bx, bx, i, ny).start()
         remote(by, by, i, nx).start()
         ag_wait_sent(i, n, name)
 
     def ag_last(name):
-        full = ffb if name == "d" else rows_chip
-        wait_in(block(name, full * qd, full), ag[name][0])
-        if name != "d":
+        wait_in(chip_rows(name, qd, 0, span(name)), ag[name][0])
+        if name[0] != "d":
             wait_in(block(name, my, rows_dev), local_i[name])
 
     flip("q")
@@ -632,6 +608,10 @@
     n_copies = []
     for k in range(2):
         wait_in(rows(xb, quarter * k, quarter), x_i + k)
+        if k == 1:
+            for m in range(2):
+                dst = rows(r["cb"], quarter * z, quarter)
+                to_chip(cot.at[m], dst, c_i + zk, c_i + m, 2 * m + c, zh)
         cen, rstd = row_stats(xb[pl.ds(quarter * k, quarter), :].astype(F32))
         normed[pl.ds(own0 + quarter * k, quarter), :] = (cen * rstd * gain_one).astype(BF)
         mine = rows(normed, own0 + quarter * k, quarter)
@@ -653,7 +633,7 @@
         copy.wait_recv()
     qkv_rows(oth0)
     ag_second("o")
-
+    ag_second("u0")
     attended, lev = r["attended"], r["lev"]
     lane = lax.broadcasted_iota(jnp.int32, (1, LANES), 1)
     head_lane = [jnp.where(lane < LANES // 2, 1.0, 0.0), jnp.where(lane < LANES // 2, 0.0, 1.0)]
@@ -683,6 +663,10 @@
                 out = tn(signed, value * head_bf[h])
                 total_out = out if total_out is None else total_out + out
             attended[qs, dcol(c * hcols + p * LANES, LANES)] = total_out.astype(BF)
+            if p == 1 and b == 1:
+                ag_second("u1")
+                ag_first("d0")
+                ag_first("d1")
 
     att_i = sems(pairs)
 
@@ -695,19 +679,9 @@
         att_copy(p).start()
         ends.append(att_copy(p).wait_send)
         if p == 0:
-            ag_second_u("u0")
             ag_last("o")
             half_o = W["o"].at[:, dcol(c * hcols, hcols)]
             o_copy = send(half_o, half_o, part)
-        if p == 1:
-            ag_second_u("u1")
-            ag_third_u("u0")
-            ag_first("d")
-        if p == 2:
-            ag_third_u("u1")
-            for m in range(2):
-                dst = rows(r["cb"], quarter * z, quarter)
-                to_chip(cot.at[m], dst, c_i + zk, c_i + m, 2 * m + c, zh)
     o_copy.wait_recv()
     for p in range(pairs):
         att_copy(p).wait_recv()
@@ -723,6 +697,13 @@
         n2[ts, :] = (cen * rstd * gain_two).astype(BF)
         mine = rows(n2, own0 + quarter * k, quarter)
         n2_copies.append(send(mine, mine, part))
+
+    cb = r["cb"]
+    c_copies = []
+    for k in range(2):
+        mine = rows(cb, own0 + quarter * k, quarter)
+        wait_in(mine, c_i + k)
+        c_copies.append(send(mine, mine, part))
 
     active, du = r["active"], r["du"]
     ft = 256
@@ -744,16 +725,16 @@
 
         lax.fori_loop(0, 2 * nft, step, 0)
 
-    ag_last_u("u0")
+    ag_last("u0")
     up_rows(own0, 0)
     for copy in n2_copies:
         copy.wait_recv()
+    ag_last("u1")
+    up_rows(own0, half_u)
+    ag_second("d0")
     up_rows(oth0, 0)
-    ag_last_u("u1")
-    up_rows(own0, half_u)
-    ag_second("d")
-    wait_in(rows(W["d"], ffb * q, ffb), local_d)
     up_rows(oth0, half_u)
+    ag_second("d1")
 
     def reduce_unit(name, ref, stride, off, n, cols, place):
         h2 = n // 2
@@ -890,7 +871,10 @@
 
     def stages():
         for at in next(turn):
-            red[units[at // 6]][at % 6]()
+            if at < 6 * len(units):
+                red[units[at // 6]][at % 6]()
+            else:
+                tokens_out(at - 6 * len(units))
 
     xs, xr, mixacc = r["xs"], r["xr"], r["mixacc"]
 
@@ -901,20 +885,29 @@
             out = nn(active[pl.ds(first + quarter * k, quarter), dcol(ffb * blk, ffb)], W["d"][w_rows, :])
             into[ls, :] = out if fresh else into[ls, :] + out
 
+    for copy in c_copies:
+        copy.wait_recv()
+    gt = 256
+
+    def grad_down_step(i, _):
+        cols = dcol(gt * i, gt)
+        r["g_d"][pl.ds(pl.multiple_of(gt * i, gt), gt), :] = tn(active[:, cols], cb[...]).astype(BF)
+        return 0
+
+    lax.fori_loop(0, ffh // gt, grad_down_step, 0)
+    wait_in(rows(W["d"], ffb * q, ffb), local_d)
+    stages()
+
     for i, blk in enumerate((q, qx, qy)):
         down(blk, oth0, xs.at[1], i == 0)
-    ag_last("d")
+    stages()
+    ag_last("d0")
+    ag_last("d1")
     down(qd, oth0, xs.at[1], False)
     mix_copies = [
         send(xs.at[1, pl.ds(quarter * k, quarter), :], xr.at[1, pl.ds(quarter * k, quarter), :], part)
         for k in range(2)
     ]
-    cb = r["cb"]
-    c_copies = []
-    for k in range(2):
-        mine = rows(cb, own0 + quarter * k, quarter)
-        wait_in(mine, c_i + k)
-        c_copies.append(send(mine, mine, part))
     for k in range(2):
         ls = pl.ds(quarter * k, quarter)
         mixacc[ls, :] = nn(active[pl.ds(own0 + quarter * k, quarter), :], W["d"][...])
@@ -948,18 +941,11 @@
         ls = pl.ds(quarter * k, quarter)
         mix_copies[k].wait_recv()
         mixb[ls, :] = (middle[ls, :] + mixacc[ls, :] + xr[1, ls, :]).astype(BF)
-        from_chip(mixb, r["o_mixed"], mo_i, k)
-
-    for copy in c_copies:
-        copy.wait_recv()
-    gt = 256
-
-    def grad_down_step(i, _):
-        cols = dcol(gt * i, gt)
-        r["g_d"][pl.ds(pl.multiple_of(gt * i, gt), gt), :] = tn(active[:, cols], cb[...]).astype(BF)
-        return 0
-
-    lax.fori_loop(0, ffh // gt, grad_down_step, 0)
+
+    def tokens_out(at):
+        buf, out, i = (mixb, r["o_mixed"], mo_i) if at < 2 else (r["gtb"], r["o_gt"], to_i)
+        from_chip(buf, out, i, at % 2)
+
     stages()
 
     fd = 512
@@ -1099,13 +1085,13 @@
     lax.fori_loop(0, width // gt, grad_out_step, 0)
     stages()
     attend_back(2)
-    grad_qkv(2)
-    stages()
 
     for copy in dn2_copies:
         copy.wait_send()
         ends.remove(copy.wait_send)
     dn1_copies = exchange(2, lambda ts: nt(qkv[ts, :], W["q"][...]))
+    stages()
+    grad_qkv(2)
     stages()
     gtb = r["gtb"]
     gain_acc = jnp.zeros((1, width), F32)
@@ -1119,7 +1105,6 @@
         n = cen * rstd
         gain_acc = gain_acc + jnp.sum(dn * n, axis=0, keepdims=True)
         gtb[ls, :] = (mixacc[ls, :] + norm_back(dn, n, rstd, gain_one)).astype(BF)
-        from_chip(gtb, r["o_gt"], to_i, k)
         stages()
     gsum[0, :, :width] = gain_acc
 

time: 176 us -> 171 us (0.972)
  the two profiles are of different devices: /device:TPU:24 before, /device:TPU:1 now
where the time goes in v1:
time: 171 us; the launch traced here: 168 us
  Pallas kernels  160 us (94%)
  other arithmetic  6.38 us (4%)
    pallas_call x1, Pallas kernels, per_device_fast(): pl.pallas_call(functools.partial(layer_kernel, names), out_shape=[jax.Sha...  160 us

profile of v1, /device:TPU:1, one launch (start us, length us, event | category | flops | bytes accessed | tf_op | source)
XLA Modules:
  0.0 168.5 jit_solution(1617923253982582150)
XLA Ops:
  0.6 159.5 %shard_map.152 = (bf16[2,256,768]{2,1,0:T(8,128)(2,1)}, bf16[2,256,768]{2,1,0:T(8,128)(2,1)}, bf16[96,2304]{1,0:T(8,128)(2,1)}, bf16[96,768]{1,0:T(8,128)(2,1)},...) custom-call(bf16[2,256,768]{2,1,0:T(8,128)(2,1)} %bitcast.18, s32[2,1,256]{2,1,0:T(1,128)} %refs_1_.1, ...), custom_call_target="tpu_custom_call" | custom-call | flops 28085059584 | bytes 15728640 | tf_op jit(solution)/shard_map/pallas_call | solution.py:1244
  160.2 0.0 copy-start.3
  160.2 0.0 copy-start.4
  160.2 0.0 copy-start.2
  160.2 2.5 %bitcast_convert_fusion = f32[2,1,256,768]{3,2,1,0:T(8,128)} fusion(bf16[2,256,768]{2,1,0:T(8,128)(2,1)} %get-tuple-element.16), kind=kLoop, calls=%fused_computation | loop fusion | flops 393216 | bytes 2359296
  162.7 0.0 copy-done.3
  162.7 0.0 copy-start.1
  162.7 1.0 convert_element_type.13
  163.7 0.0 copy-done.4
  163.7 0.7 convert_element_type.14
  164.4 0.0 copy-done.2
  164.4 0.0 copy-start.5
  164.4 0.0 copy-start
  164.4 1.1 convert_element_type.15
  165.5 0.0 copy-done.1
  165.5 1.1 convert_element_type.16
  166.6 0.0 copy-done.5
  166.6 0.5 slice_bitcast_fusion
  167.1 0.0 copy-done
  167.2 0.9 copy.20
Async XLA Ops:
  160.2 2.5 %copy-start.3 = (bf16[96,2304]{1,0:T(8,128)(2,1)S(1)}, bf16[96,2304]{1,0:T(8,128)(2,1)}, u32[]{:S(2)}) copy-start(bf16[96,2304]{1,0:T(8,128)(2,1)} %get-tuple-element.17) | copy-start | bytes 1327108
  160.2 3.5 %copy-start.4 = (bf16[96,768]{1,0:T(8,128)(2,1)S(1)}, bf16[96,768]{1,0:T(8,128)(2,1)}, u32[]{:S(2)}) copy-start(bf16[96,768]{1,0:T(8,128)(2,1)} %get-tuple-element.18) | copy-start | bytes 442372
  160.2 4.2 %copy-start.2 = (bf16[96,3072]{1,0:T(8,128)(2,1)S(1)}, bf16[96,3072]{1,0:T(8,128)(2,1)}, u32[]{:S(2)}) copy-start(bf16[96,3072]{1,0:T(8,128)(2,1)} %get-tuple-element.19) | copy-start | bytes 1769476
  162.7 2.8 %copy-start.1 = (bf16[384,768]{1,0:T(8,128)(2,1)S(1)}, bf16[384,768]{1,0:T(8,128)(2,1)}, u32[]{:S(2)}) copy-start(bf16[384,768]{1,0:T(8,128)(2,1)} %get-tuple-element.20) | copy-start | bytes 1769476
  164.4 2.2 %copy-start.5 = (f32[2,96]{1,0:T(2,128)S(1)}, f32[2,96]{1,0:T(2,128)}, u32[]{:S(2)}) copy-start(f32[2,96]{1,0:T(2,128)} %get-tuple-element.21) | copy-start | bytes 2308
  164.4 2.7 %copy-start = (bf16[2,256,768]{2,1,0:T(8,128)(2,1)S(1)}, bf16[2,256,768]{2,1,0:T(8,128)(2,1)}, u32[]{:S(2)}) copy-start(bf16[2,256,768]{2,1,0:T(8,128)(2,1)} %get-tuple-element.15) | copy-start | bytes 2359300

commit v2 on v1

--- a/solution.py
+++ b/solution.py
@@ -285,14 +285,14 @@
     (44, 33, 55, 17,),
     (28,),
     (39, 61, 66, 23,),
-    (49, 45, 34, 74,),
-    (56, 29, 75,),
-    (62, 40, 35,),
-    (67, 46, 50, 68,),
-    (57, 41, 63,),
-    (47, 51, 58, 69,),
-    (64, 59, 52,),
-    (65, 70, 53, 71,),
+    (49, 45, 34,),
+    (56, 29,),
+    (62, 40, 74, 75,),
+    (35, 67, 46, 76, 50,),
+    (57, 41, 68, 63, 47,),
+    (58, 77, 78, 51, 64,),
+    (59, 69, 52, 79, 65,),
+    (80, 70, 81, 53, 71,),
 )
 
 HUGE = 3.0e38
@@ -912,12 +912,12 @@
         ls = pl.ds(quarter * k, quarter)
         mixacc[ls, :] = nn(active[pl.ds(own0 + quarter * k, quarter), :], W["d"][...])
 
-    def from_chip(buf, out, i0, k):
+    def from_chip(buf, out, i0, k, first, n, last):
         zd = 2 * c + k
-        src = buf.at[pl.ds(quarter * k, quarter), :]
+        src = buf.at[pl.ds(quarter * k + first, n), :]
         is_self = (zd == z) & (zk == c)
         dev = (zd, s - c + zk)
-        dst = out.at[zh]
+        dst = out.at[zh, pl.ds(first, n), :]
 
         @pl.when(is_self)
         def _():
@@ -930,10 +930,12 @@
         def end():
             @pl.when(jnp.logical_not(is_self))
             def _():
-                remote(src, dst, i0 + zh, dev, i0 + k).wait_send()
-
-        ends.append(end)
-        waits.append(functools.partial(wait_in, out.at[k], i0 + k))
+                whole = buf.at[pl.ds(quarter * k, quarter), :]
+                remote(whole, out.at[zh], i0 + zh, dev, i0 + k).wait_send()
+
+        if last:
+            ends.append(end)
+            waits.append(functools.partial(wait_in, out.at[k], i0 + k))
 
     mo_i, to_i = sems(2), sems(2)
     mixb = r["mixb"]
@@ -943,8 +945,11 @@
         mixb[ls, :] = (middle[ls, :] + mixacc[ls, :] + xr[1, ls, :]).astype(BF)
 
     def tokens_out(at):
-        buf, out, i = (mixb, r["o_mixed"], mo_i) if at < 2 else (r["gtb"], r["o_gt"], to_i)
-        from_chip(buf, out, i, at % 2)
+        if at < 2:
+            from_chip(mixb, r["o_mixed"], mo_i, at, 0, quarter, True)
+        else:
+            piece, n = at - 2, quarter // 4
+            from_chip(r["gtb"], r["o_gt"], to_i, piece // 4, piece % 4 * n, n, piece % 4 == 3)
 
     stages()
 

time: 171 us -> 169 us (0.988)
  the two profiles are of different devices: /device:TPU:1 before, /device:TPU:24 now
where the time goes in v2:
time: 169 us; the launch traced here: 167 us
  Pallas kernels  158 us (93%)
  other arithmetic  6.38 us (4%)
    pallas_call x1, Pallas kernels, per_device_fast(): pl.pallas_call(functools.partial(layer_kernel, names), out_shape=[jax.Sha...  158 us

profile of v2, /device:TPU:24, one launch (start us, length us, event | category | flops | bytes accessed | tf_op | source)
XLA Modules:
  0.0 166.7 jit_solution(10282053873916928758)
XLA Ops:
  0.6 157.8 %shard_map.152 = (bf16[2,256,768]{2,1,0:T(8,128)(2,1)}, bf16[2,256,768]{2,1,0:T(8,128)(2,1)}, bf16[96,2304]{1,0:T(8,128)(2,1)}, bf16[96,768]{1,0:T(8,128)(2,1)},...) custom-call(bf16[2,256,768]{2,1,0:T(8,128)(2,1)} %bitcast.18, s32[2,1,256]{2,1,0:T(1,128)} %refs_1_.1, ...), custom_call_target="tpu_custom_call" | custom-call | flops 28085059584 | bytes 15728640 | tf_op jit(solution)/shard_map/pallas_call | solution.py:1249
  158.5 0.0 copy-start.3
  158.5 0.0 copy-start.4
  158.5 0.0 copy-start.2
  158.5 2.5 %bitcast_convert_fusion = f32[2,1,256,768]{3,2,1,0:T(8,128)} fusion(bf16[2,256,768]{2,1,0:T(8,128)(2,1)} %get-tuple-element.16), kind=kLoop, calls=%fused_computation | loop fusion | flops 393216 | bytes 2359296
  161.0 0.0 copy-done.3
  161.0 0.0 copy-start.1
  161.0 1.0 convert_element_type.13
  161.9 0.0 copy-done.4
  162.0 0.7 convert_element_type.14
  162.7 0.0 copy-done.2
  162.7 0.0 copy-start.5
  162.7 0.0 copy-start
  162.7 1.1 convert_element_type.15
  163.8 0.0 copy-done.1
  163.8 1.1 convert_element_type.16
  164.9 0.0 copy-done.5
  164.9 0.5 slice_bitcast_fusion
  165.4 0.0 copy-done
  165.4 0.9 copy.20
Async XLA Ops:
  158.5 2.5 %copy-start.3 = (bf16[96,2304]{1,0:T(8,128)(2,1)S(1)}, bf16[96,2304]{1,0:T(8,128)(2,1)}, u32[]{:S(2)}) copy-start(bf16[96,2304]{1,0:T(8,128)(2,1)} %get-tuple-element.17) | copy-start | bytes 1327108
  158.5 3.5 %copy-start.4 = (bf16[96,768]{1,0:T(8,128)(2,1)S(1)}, bf16[96,768]{1,0:T(8,128)(2,1)}, u32[]{:S(2)}) copy-start(bf16[96,768]{1,0:T(8,128)(2,1)} %get-tuple-element.18) | copy-start | bytes 442372
  158.5 4.2 %copy-start.2 = (bf16[96,3072]{1,0:T(8,128)(2,1)S(1)}, bf16[96,3072]{1,0:T(8,128)(2,1)}, u32[]{:S(2)}) copy-start(bf16[96,3072]{1,0:T(8,128)(2,1)} %get-tuple-element.19) | copy-start | bytes 1769476
  161.0 2.8 %copy-start.1 = (bf16[384,768]{1,0:T(8,128)(2,1)S(1)}, bf16[384,768]{1,0:T(8,128)(2,1)}, u32[]{:S(2)}) copy-start(bf16[384,768]{1,0:T(8,128)(2,1)} %get-tuple-element.20) | copy-start | bytes 1769476
  162.7 2.2 %copy-start.5 = (f32[2,96]{1,0:T(2,128)S(1)}, f32[2,96]{1,0:T(2,128)}, u32[]{:S(2)}) copy-start(f32[2,96]{1,0:T(2,128)} %get-tuple-element.21) | copy-start | bytes 2308
  162.7 2.7 %copy-start = (bf16[2,256,768]{2,1,0:T(8,128)(2,1)S(1)}, bf16[2,256,768]{2,1,0:T(8,128)(2,1)}, u32[]{:S(2)}) copy-start(bf16[2,256,768]{2,1,0:T(8,128)(2,1)} %get-tuple-element.15) | copy-start | bytes 2359300

commit v3 on v2

--- a/solution.py
+++ b/solution.py
@@ -268,31 +268,31 @@
     (8, 24, 30,),
     (14,),
     (20, 36,),
+    (3,),
+    (25,),
     (),
-    (3, 25,),
-    (42,),
-    (9, 31,),
+    (9, 42, 31,),
     (),
-    (15, 4,),
-    (37,),
-    (21, 26, 54,),
-    (10,),
-    (43, 5,),
-    (32, 16, 60,),
-    (38,),
-    (27, 22,),
-    (48, 11,),
-    (44, 33, 55, 17,),
+    (15, 37, 4,),
+    (),
+    (26, 48,),
+    (21, 10,),
+    (43, 16, 5,),
+    (32, 54,),
+    (27, 38,),
+    (22, 11,),
+    (60,),
+    (44, 33, 49, 17,),
     (28,),
-    (39, 61, 66, 23,),
-    (49, 45, 34,),
-    (56, 29,),
-    (62, 40, 74, 75,),
-    (35, 67, 46, 76, 50,),
-    (57, 41, 68, 63, 47,),
-    (58, 77, 78, 51, 64,),
-    (59, 69, 52, 79, 65,),
-    (80, 70, 81, 53, 71,),
+    (39, 55, 66, 23,),
+    (61, 45, 34,),
+    (50, 29,),
+    (56, 40, 74, 75,),
+    (35, 67, 46, 76, 62,),
+    (51, 41, 68, 57, 47,),
+    (52, 77, 78, 63, 58,),
+    (53, 69, 64, 79, 59,),
+    (80, 70, 81, 65, 71,),
 )
 
 HUGE = 3.0e38
@@ -1081,13 +1081,13 @@
         r["g_o"][pl.ds(pl.multiple_of(gt * i, gt), gt), :] = out
         return 0
 
+    lax.fori_loop(0, width // gt, grad_out_step, 0)
+    stages()
     attend_back(0)
     grad_qkv(0)
     stages()
     attend_back(1)
     grad_qkv(1)
-    stages()
-    lax.fori_loop(0, width // gt, grad_out_step, 0)
     stages()
     attend_back(2)
 

time: 169 us -> 169 us (level)
  no operation moved by 1% of the time
where the time goes in v3:
time: 169 us; the launch traced here: 167 us
  Pallas kernels  158 us (93%)
  other arithmetic  6.38 us (4%)
    pallas_call x1, Pallas kernels, per_device_fast(): pl.pallas_call(functools.partial(layer_kernel, names), out_shape=[jax.Sha...  158 us

profile of v3, /device:TPU:24, one launch (start us, length us, event | category | flops | bytes accessed | tf_op | source)
XLA Modules:
  0.0 166.7 jit_solution(486809385159465671)
XLA Ops:
  0.6 157.8 %shard_map.152 = (bf16[2,256,768]{2,1,0:T(8,128)(2,1)}, bf16[2,256,768]{2,1,0:T(8,128)(2,1)}, bf16[96,2304]{1,0:T(8,128)(2,1)}, bf16[96,768]{1,0:T(8,128)(2,1)},...) custom-call(bf16[2,256,768]{2,1,0:T(8,128)(2,1)} %bitcast.18, s32[2,1,256]{2,1,0:T(1,128)} %refs_1_.1, ...), custom_call_target="tpu_custom_call" | custom-call | flops 28085059584 | bytes 15728640 | tf_op jit(solution)/shard_map/pallas_call | solution.py:1249
  158.5 0.0 copy-start.3
  158.5 0.0 copy-start.4
  158.5 0.0 copy-start.2
  158.5 2.5 %bitcast_convert_fusion = f32[2,1,256,768]{3,2,1,0:T(8,128)} fusion(bf16[2,256,768]{2,1,0:T(8,128)(2,1)} %get-tuple-element.16), kind=kLoop, calls=%fused_computation | loop fusion | flops 393216 | bytes 2359296
  161.0 0.0 copy-done.3
  161.0 0.0 copy-start.1
  161.0 1.0 convert_element_type.13
  161.9 0.0 copy-done.4
  161.9 0.7 convert_element_type.14
  162.7 0.0 copy-done.2
  162.7 0.0 copy-start.5
  162.7 0.0 copy-start
  162.7 1.1 convert_element_type.15
  163.8 0.0 copy-done.1
  163.8 1.1 convert_element_type.16
  164.9 0.0 copy-done.5
  164.9 0.5 slice_bitcast_fusion
  165.4 0.0 copy-done
  165.4 0.9 copy.20
Async XLA Ops:
  158.5 2.5 %copy-start.3 = (bf16[96,2304]{1,0:T(8,128)(2,1)S(1)}, bf16[96,2304]{1,0:T(8,128)(2,1)}, u32[]{:S(2)}) copy-start(bf16[96,2304]{1,0:T(8,128)(2,1)} %get-tuple-element.17) | copy-start | bytes 1327108
  158.5 3.5 %copy-start.4 = (bf16[96,768]{1,0:T(8,128)(2,1)S(1)}, bf16[96,768]{1,0:T(8,128)(2,1)}, u32[]{:S(2)}) copy-start(bf16[96,768]{1,0:T(8,128)(2,1)} %get-tuple-element.18) | copy-start | bytes 442372
  158.5 4.2 %copy-start.2 = (bf16[96,3072]{1,0:T(8,128)(2,1)S(1)}, bf16[96,3072]{1,0:T(8,128)(2,1)}, u32[]{:S(2)}) copy-start(bf16[96,3072]{1,0:T(8,128)(2,1)} %get-tuple-element.19) | copy-start | bytes 1769476
  161.0 2.8 %copy-start.1 = (bf16[384,768]{1,0:T(8,128)(2,1)S(1)}, bf16[384,768]{1,0:T(8,128)(2,1)}, u32[]{:S(2)}) copy-start(bf16[384,768]{1,0:T(8,128)(2,1)} %get-tuple-element.20) | copy-start | bytes 1769476
  162.7 2.2 %copy-start.5 = (f32[2,96]{1,0:T(2,128)S(1)}, f32[2,96]{1,0:T(2,128)}, u32[]{:S(2)}) copy-start(f32[2,96]{1,0:T(2,128)} %get-tuple-element.21) | copy-start | bytes 2308
  162.7 2.7 %copy-start = (bf16[2,256,768]{2,1,0:T(8,128)(2,1)S(1)}, bf16[2,256,768]{2,1,0:T(8,128)(2,1)}, u32[]{:S(2)}) copy-start(bf16[2,256,768]{2,1,0:T(8,128)(2,1)} %get-tuple-element.15) | copy-start | bytes 2359300
